TPU v7x, 256 devices: a whole 4x4x8 slice. The times are simulated.
256 devices in a mesh: tile: 128 (over y, z_hi, x, core), lev: 2 (over z_lo).
Axes of the slice: x: 4, y: 4, z: 8 (z_hi: 4, z_lo: 2; z = z_hi * 2 + z_lo), core: 2. Of those that a mesh axis runs over, the one named last changes fastest.
Arguments:
- fields: float32 [4, 64, 2048, 128], P(None, 'lev', 'tile'), may hold values from -6 to 6
- horizontal_mix: float32 [64, 2048, 128], P('lev', 'tile'), may hold values from 0.1 to 0.2
- vertical_mix: float32 [64, 2048, 128], P('lev', 'tile'), may hold values from 0.03 to 0.07
- edge_flip: int32 [128], replicated, may hold values 0 or 1
- batch_slots: int32 [128, 128, 16], replicated, may hold values from -1 to 2047, as said below
- w_first: bfloat16 [4, 64, 768], replicated, may hold values from -1 to 1
- bias_first: float32 [768], replicated, may hold values from -3 to 3
- w_middle: bfloat16 [4, 768, 768], replicated, may hold values from -0.375 to 0.375
- bias_middle: float32 [4, 768], replicated, may hold values from -3 to 3
- w_output: bfloat16 [768, 4, 64], P(None, None, 'lev'), may hold values from -0.21875 to 0.21875
Outputs:
- advanced: float32 [4, 64, 2048, 128], P(None, 'lev', 'tile')
- tendency: bfloat16 [4, 64, 2048, 128], P(None, 'lev', 'tile')
Inputs may be any that keep to these rules, and one draw needn't show every extreme that they name: Each tile's entries batch_slots[s] are either all -1 (an inactive tile) or hold each of its 2048 cell numbers exactly once; exactly 32 tiles are active. Entry [s, b, j] places a cell of tile s in slot j of physics batch b, so every batch receives exactly 16 columns from every active tile.
All inputs are finite; a program needn't handle non-finite values.
Results may differ from a plain program's by a relative error of at most 0.01.
Values may be sent and summed in bfloat16 or wider, within the bound.
No kernel may reach another device: no remote copies, remote signals or barrier semaphores. Data moves between devices by JAX's collectives and lax.ppermute only.
A program may use at most 64 MiB of HBM per device.

v0:
```python
from functools import partial

import jax
import jax.numpy as jnp
from jax import lax
from jax.sharding import PartitionSpec as P

SUB = 3


def padded_2(shard, sides, width, wrap):
    for axis, dim in sides:
        count, length = (lax.axis_size(axis), shard.shape[dim])
        up = [(i, (i + 1) % count) for i in range(count if wrap else count - 1)]
        down = [(j, i) for i, j in up]
        last = lax.slice_in_dim(shard, length - width, length, axis=dim)
        initial = lax.slice_in_dim(shard, 0, width, axis=dim)
        before = lax.ppermute(last, axis, up)
        after = lax.ppermute(initial, axis, down)
        shard = jnp.concatenate([before, shard, after], axis=dim)
    return shard


def mirror_rims(padded, edge_flip, width):
    count = lax.axis_size("tile")
    place = lax.axis_index("tile")
    flip_west = edge_flip[place] > 0
    flip_east = edge_flip[(place + 1) % count] > 0
    span = padded.shape[2]
    west_rim = padded[:, :, :width]
    east_rim = padded[:, :, span - width :]
    middle = padded[:, :, width : span - width]
    west_rim = jnp.where(flip_west, west_rim[..., ::-1], west_rim)
    east_rim = jnp.where(flip_east, east_rim[..., ::-1], east_rim)
    return jnp.concatenate([west_rim, middle, east_rim], axis=2)


def level_rims(block):
    return padded_2(block, (("lev", 1),), 1, False)


def advance_region(padded, mix_pad, vertical_lev):
    centre = padded[:, 1:-1, 1:-1]
    west_side = padded[:, 1:-1, :-2]
    east_side = padded[:, 1:-1, 2:]
    above = padded[:, 2:, 1:-1]
    below = padded[:, :-2, 1:-1]
    mix_centre = mix_pad[:, 1:-1]
    change = 0.5 * (mix_centre + mix_pad[:, :-2]) * (west_side - centre)
    change = change + 0.5 * (mix_centre + mix_pad[:, 2:]) * (east_side - centre)
    change = change + 0.5 * (mix_centre + jnp.roll(mix_centre, -1, axis=2)) * (
        jnp.roll(centre, -1, axis=3) - centre
    )
    change = change + 0.5 * (mix_centre + jnp.roll(mix_centre, 1, axis=2)) * (
        jnp.roll(centre, 1, axis=3) - centre
    )
    vertical_centre = vertical_lev[1:-1]
    change = change + 0.5 * (vertical_centre + vertical_lev[2:]) * (above - centre)
    change = change + 0.5 * (vertical_centre + vertical_lev[:-2]) * (below - centre)
    return centre + change


def add_levels(w_first, total, piece, start):
    return jnp.einsum("rfk,fkh->rh", piece, w_first, preferred_element_type=jnp.float32)


def first_layer(batch, w_first):
    empty = jnp.zeros((batch.shape[0], w_first.shape[2]), jnp.float32)
    adder = partial(add_levels, w_first)
    return adder(empty, lax.all_gather(batch, "lev", axis=2, tiled=True), jnp.int32(0))


def column_net(batch, w_first, bias_first, w_middle, bias_middle, w_output):
    hidden = jax.nn.silu(first_layer(batch, w_first) + bias_first).astype(jnp.bfloat16)
    for layer in range(w_middle.shape[0]):
        hidden = jnp.dot(hidden, w_middle[layer], preferred_element_type=jnp.float32)
        hidden = jax.nn.silu(hidden + bias_middle[layer]).astype(jnp.bfloat16)
    result = jnp.dot(
        hidden, w_output.reshape(w_output.shape[0], -1), preferred_element_type=jnp.float32
    )
    return result.astype(jnp.bfloat16)


def on_device(
    fields,
    horizontal_mix,
    vertical_mix,
    edge_flip,
    batch_slots,
    w_first,
    bias_first,
    w_middle,
    bias_middle,
    w_output,
):
    stacked = jnp.concatenate([fields, horizontal_mix[None], vertical_mix[None]], axis=0)
    extended = mirror_rims(padded_2(stacked, (("tile", 2),), 1, True), edge_flip, 1)
    mix_full = extended[4]
    vertical_full = extended[5]
    current = extended[:4]
    vertical_levels = vertical_full
    for step in range(SUB):
        if step > 0:
            current = mirror_rims(padded_2(current, (("tile", 2),), 1, True), edge_flip, 1)
        if step == 0:
            lifted = level_rims(jnp.concatenate([current, vertical_full[None]], axis=0))
            vertical_levels = lifted[4]
            current_levels = lifted[:4]
        else:
            current_levels = level_rims(current)
        region = current.shape[2]
        vertical_lev = vertical_levels[:, 1 : region - 1]
        current = advance_region(current_levels, mix_full, vertical_lev)
    place = lax.axis_index("tile")
    half = fields.shape[1]
    width_x = fields.shape[2]
    width_y = fields.shape[3]
    cells = width_x * width_y
    profiles = current.astype(jnp.bfloat16).transpose(2, 3, 0, 1).reshape(cells, 4 * half)
    my_slots = batch_slots[place]
    valid = my_slots >= 0
    target = jnp.where(valid, my_slots, cells).reshape(-1)
    results = column_net(
        profiles.reshape(cells, 4, half), w_first, bias_first, w_middle, bias_middle, w_output
    )
    active = jnp.zeros((cells + 1,), jnp.int32).at[target].set(1)[:cells]
    tendency_cells = jnp.where(active[:, None] > 0, results, jnp.zeros((), jnp.bfloat16))
    tendency = tendency_cells.reshape(width_x, width_y, 4, half).transpose(2, 3, 0, 1)
    return (current, tendency)


def solution(mesh):
    return jax.shard_map(
        on_device,
        mesh=mesh,
        in_specs=(
            P(None, "lev", "tile", None),
            P("lev", "tile", None),
            P("lev", "tile", None),
            P(),
            P(),
            P(),
            P(),
            P(),
            P(),
            P(None, None, "lev"),
        ),
        out_specs=(P(None, "lev", "tile", None), P(None, "lev", "tile", None)),
        check_vma=False,
    )
```

profile of v0, /device:TPU:24, one launch (start us, length us, event | category | flops | bytes accessed | tf_op | source)
XLA Modules:
  0.0 145.2 jit_solution(6975538116259365410)
XLA Ops:
  7.2 0.0 copy-start
  7.2 0.0 copy-start.1
  7.2 0.0 all-gather.2.cloned.1.call-start
  7.2 1.8 %pad_maximum_fusion.33 = (f32[6,32,1,128]{3,2,1,0:T(1,128)S(1)}, f32[6,32,1,128]{3,2,1,0:T(1,128)S(1)}) fusion(f32[1,32,16,128]{3,2,1,0:T(8,128)} %bitcast.67, f32[1,32,16,128]{3,2,1,0:T(8,128)} %bitcast.71, f32[4,32,16,128]{3,2,1,0:T(8,128)} %param.10), kind=kLoop, calls=%fused_computation.125 | loop fusion | flops 98304 | bytes 1769472 | tf_op jit(solution)/shard_map/slice | solution.py:16
  9.0 0.1 collective-permute-start
  9.1 0.0 copy-start.2
  9.1 0.0 copy-start.3
  9.1 8.2 %collective-permute-start.1 = (f32[6,32,1,128]{3,2,1,0:T(1,128)S(1)}, f32[6,32,1,128]{3,2,1,0:T(1,128)S(1)}, u32[]{:S(2)}, u32[]{:S(2)}) collective-permute-start(f32[6,32,1,128]{3,2,1,0:T(1,128)S(1)} %get-tuple-element.13), channel_id=1, source_target_pairs={{2,0},{4,2},{6,4},{8,6},{10,8},{12,10},{14,12},{16,14},{18,16},{20... | collective-permute-start | bytes 294920 | tf_op jit(solution)/shard_map/ppermute | solution.py:19
  17.3 3.2 %fusion.80 = (f32[4,32,16,1]{3,2,1,0:T(8,128)}, f32[4,32,16,1]{3,2,1,0:T(8,128)}) fusion(f32[4,32,16,128]{3,2,1,0:T(8,128)} %param.10), kind=kLoop, calls=%fused_computation.153 | loop fusion | bytes 32768 | tf_op jit(solution)/shard_map/jit(_roll_static)/slice | solution.py:55
  20.5 1.6 %fusion.81 = (f32[4,32,16,127]{3,2,1,0:T(8,128)}, f32[4,32,16,127]{3,2,1,0:T(8,128)}) fusion(f32[4,32,16,128]{3,2,1,0:T(8,128)S(1)} %copy-done.1), kind=kLoop, calls=%fused_computation.154 | loop fusion | bytes 4161536 | tf_op jit(solution)/shard_map/jit(_roll_static)/slice | solution.py:55
  22.2 0.6 fusion.84
  24.0 0.7 rev.18
  24.7 0.7 rev.19
  25.5 0.1 maximum_bitcast_fusion
  25.6 0.1 fusion.82
  25.8 0.1 fusion.83
  25.9 0.4 pad_maximum_fusion
  26.3 0.1 slice.315
  26.4 0.0 copy-start.4
  26.4 0.0 copy-start.9
  26.5 3.2 %collective-permute-start.2 = (f32[5,1,18,128]{3,2,1,0:T(8,128)S(1)}, f32[5,1,18,128]{3,2,1,0:T(8,128)S(1)}, u32[]{:S(2)}, u32[]{:S(2)}) collective-permute-start(f32[5,1,18,128]{3,2,1,0:T(8,128)S(1)} %get-tuple-element.9), channel_id=1, source_target_pairs={{0,1},{2,3},{4,5},{6,7},{8,9},{10,11},{12,13},{14,15},{16,17},{18,... | collective-permute-start | bytes 138248 | tf_op jit(solution)/shard_map/ppermute | solution.py:18
  29.7 1.3 collective-permute-start.3
  31.0 0.2 fusion.65
  31.2 0.3 collective-permute-done.2
  31.5 4.3 %collective-permute-done.3 = f32[5,1,18,128]{3,2,1,0:T(8,128)S(1)} collective-permute-done((f32[5,1,18,128]{3,2,1,0:T(8,128)S(1)}, f32[5,1,18,128]{3,2,1,0:T(8,128)S(1)}, u32[]{:S(2)}, u32[]{:S(2)}) %collective-permute-start.3) | collective-permute-done | bytes 46112 | tf_op jit(solution)/shard_map/ppermute | solution.py:19
  35.9 2.2 %fusion.44 = f32[4,32,16,128]{3,2,1,0:T(8,128)S(1)} fusion(f32[4,32,16,128]{3,2,1,0:T(8,128)S(1)} %copy-done.1, f32[5,1,18,128]{3,2,1,0:T(8,128)S(1)} %collective-permute-done.2, f32[1,32,18,128]{3,2,1,0:T(8,128)S(1)} %get-tuple-element.11, f32[4,32,18,128]{3,2,1,0:T(8,128)S(1)} %slice.315, f32[5,1,18,128]{3,2,1,0:T(8,128)S(1)} %collective-permute-done.3, ...), kind=kLoop, calls=%fused_computation.66 | loop fusion | flops 7864320 | bytes 8054784 | tf_op jit(solution)/shard_map/add | solution.py:60
  38.2 0.1 fusion.79
  38.3 0.1 collective-permute-start.4
  38.4 1.7 %fusion.77 = (f32[4,32,16,1]{3,2,1,0:T(8,128)}, f32[4,32,16,1]{3,2,1,0:T(8,128)}) fusion(f32[4,32,16,128]{3,2,1,0:T(8,128)S(1)} %fusion.44), kind=kLoop, calls=%fused_computation.150 | loop fusion | bytes 32768 | tf_op jit(solution)/shard_map/jit(_roll_static)/slice | solution.py:55
  40.1 6.8 %collective-permute-start.5 = (f32[4,32,1,128]{3,2,1,0:T(1,128)S(1)}, f32[4,32,1,128]{3,2,1,0:T(1,128)S(1)}, u32[]{:S(2)}, u32[]{:S(2)}) collective-permute-start(f32[4,32,1,128]{3,2,1,0:T(1,128)S(1)} %get-tuple-element.29), channel_id=1, source_target_pairs={{2,0},{4,2},{6,4},{8,6},{10,8},{12,10},{14,12},{16,14},{18,16},{20... | collective-permute-start | bytes 196616 | tf_op jit(solution)/shard_map/ppermute | solution.py:19
  46.9 0.3 collective-permute-done.4
  47.2 0.3 rev.20
  47.5 1.3 collective-permute-done.5
  48.8 0.3 rev.21
  49.2 1.4 collective-permute-start.6
  50.6 4.5 %collective-permute-start.7 = (f32[4,1,18,128]{3,2,1,0:T(8,128)S(1)}, f32[4,1,18,128]{3,2,1,0:T(8,128)S(1)}, u32[]{:S(2)}, u32[]{:S(2)}) collective-permute-start(f32[4,1,18,128]{3,2,1,0:T(8,128)S(1)} %get-tuple-element.17), channel_id=1, source_target_pairs={{0,1},{2,3},{4,5},{6,7},{8,9},{10,11},{12,13},{14,15},{16,17},{18,... | collective-permute-start | bytes 110600 | tf_op jit(solution)/shard_map/ppermute | solution.py:18
  55.1 0.3 fusion.78
  55.5 1.4 collective-permute-done.7
  56.9 3.1 %fusion.30 = f32[4,32,16,128]{3,2,1,0:T(8,128)S(1)} fusion(f32[4,32,16,128]{3,2,1,0:T(8,128)S(1)} %fusion.44, f32[4,1,18,128]{3,2,1,0:T(8,128)S(1)} %collective-permute-done.7, f32[4,32,1,128]{3,2,1,0:T(1,128)S(1)} %bitcast.89, f32[4,32,1,128]{3,2,1,0:T(1,128)S(1)} %bitcast.87, f32[4,1,18,128]{3,2,1,0:T(8,128)S(1)} %collective-permute-done.6, ...), kind=kLoop, calls=%fused_computation.44 | loop fusion | flops 7340032 | bytes 5971968 | tf_op jit(solution)/shard_map/add | solution.py:60
  60.0 0.7 fusion.76
  60.8 0.1 collective-permute-start.8
  60.8 1.7 %fusion.74 = (f32[4,32,16,127]{3,2,1,0:T(8,128)}, f32[4,32,16,127]{3,2,1,0:T(8,128)}) fusion(f32[4,32,16,128]{3,2,1,0:T(8,128)S(1)} %fusion.30), kind=kLoop, calls=%fused_computation.147 | loop fusion | bytes 4161536 | tf_op jit(solution)/shard_map/jit(_roll_static)/slice | solution.py:52
  62.5 6.8 %collective-permute-start.9 = (f32[4,32,1,128]{3,2,1,0:T(1,128)}, f32[4,32,1,128]{3,2,1,0:T(1,128)S(1)}, u32[]{:S(2)}, u32[]{:S(2)}) collective-permute-start(f32[4,32,1,128]{3,2,1,0:T(1,128)} %get-tuple-element.23), channel_id=1, source_target_pairs={{2,0},{4,2},{6,4},{8,6},{10,8},{12,10},{14,12},{16,14},{18,16},{20... | collective-permute-start | bytes 196616 | tf_op jit(solution)/shard_map/ppermute | solution.py:19
  69.4 0.3 collective-permute-done.8
  69.6 0.9 rev.22
  70.5 0.9 broadcast_select_fusion.4
  71.4 0.2 collective-permute-done.9
  71.6 0.9 rev.23
  72.5 1.4 collective-permute-start.10
  74.0 4.5 %collective-permute-start.11 = (f32[4,1,18,128]{3,2,1,0:T(8,128)S(1)}, f32[4,1,18,128]{3,2,1,0:T(8,128)S(1)}, u32[]{:S(2)}, u32[]{:S(2)}) collective-permute-start(f32[4,1,18,128]{3,2,1,0:T(8,128)S(1)} %get-tuple-element.15), channel_id=1, source_target_pairs={{0,1},{2,3},{4,5},{6,7},{8,9},{10,11},{12,13},{14,15},{16,17},{18,... | collective-permute-start | bytes 110600 | tf_op jit(solution)/shard_map/ppermute | solution.py:18
  78.5 0.3 fusion.75
  78.9 1.4 collective-permute-done.11
  80.3 2.9 %convert_bitcast_fusion = (bf16[16,128,4,32]{1,0,3,2:T(8,128)(2,1)}, f32[4,32,16,128]{3,2,1,0:T(8,128)}) fusion(f32[4,32,16,128]{3,2,1,0:T(8,128)S(1)} %fusion.30, f32[4,32,1,128]{3,2,1,0:T(1,128)S(1)} %bitcast.85, f32[4,32,1,128]{3,2,1,0:T(1,128)S(1)} %bitcast.83, f32[4,1,18,128]{3,2,1,0:T(8,128)S(1)} %collective-permute-done.11, ...), kind=kLoop, calls=%fused_computation.98 | loop fusion | flops 7602176 | bytes 6496256 | tf_op jit(solution)/shard_map/transpose | solution.py:119
  83.2 2.1 %reshape_reshape.3 = bf16[2048,4,32]{0,2,1:T(8,128)(2,1)} reshape(bf16[16,128,4,32]{1,0,3,2:T(8,128)(2,1)} %get-tuple-element.6) | data formatting | bytes 1048576 | tf_op jit(solution)/shard_map/reshape;reshape | solution.py:124
  85.2 0.0 all-gather.2.cloned.1.call-update
  85.3 0.1 copy.13
  85.4 0.1 squeeze.29
  85.5 8.1 %scatter_custom_fusion = s32[2049]{0:T(1024)S(1)} fusion(s32[2048]{0:T(1024)S(1)} %bitcast.103, s32[2048]{0:T(1024)S(1)} %broadcast.50, s32[]{:T(128)} %constant.39.clone.1), kind=kCustom, calls=%fused_computation.137 | custom fusion | bytes 8200 | tf_op jit(solution)/shard_map/scatter | solution.py:126
  93.7 20.8 %all-gather.2.cloned.1.call-done = bf16[2048,4,64]{0,2,1:T(8,128)(2,1)} async-done(((bf16[2048,4,32]{0,2,1:T(8,128)(2,1)}), bf16[2048,4,64]{0,2,1:T(8,128)(2,1)}) %all-gather.2.cloned.1.call-update) | async-done | bytes 1048592 | tf_op jit(solution)/shard_map/all_gather | solution.py:70
  114.5 7.1 %multiply_convert_fusion.3 = bf16[2048,768]{1,0:T(8,128)(2,1)} fusion(f32[768]{0:T(1024)S(1)} %get-tuple-element.4, bf16[4,768,768]{2,1,0:T(8,128)(2,1)} %param.17, bf16[2048,4,64]{0,2,1:T(8,128)(2,1)} %all-gather.2.cloned.1.call-done, bf16[4,64,768]{2,1,0:T(8,128)(2,1)} %param.15, f32[768]{0:T(1024)S(1)} %copy-done.29), kind=kOutput, calls=%fused_computation.5 | convolution fusion | flops 3240099840 | bytes 5773312 | tf_op jit(solution)/shard_map/dot_general | solution.py:76
  121.6 9.4 %multiply_convert_fusion.1 = bf16[2048,768]{1,0:T(8,128)(2,1)} fusion(f32[768]{0:T(1024)S(1)} %get-tuple-element.5, bf16[4,768,768]{2,1,0:T(8,128)(2,1)} %param.17, bf16[2048,768]{1,0:T(8,128)(2,1)} %multiply_convert_fusion.3, f32[768]{0:T(1024)S(1)} %get-tuple-element.3), kind=kOutput, calls=%fused_computation.3 | convolution fusion | flops 4850712576 | bytes 8656896 | tf_op jit(solution)/shard_map/dot_general | solution.py:76
  131.0 6.2 %fusion = bf16[2048,128]{1,0:T(8,128)(2,1)S(1)} fusion(bf16[768,128]{0,1:T(8,128)(2,1)S(1)} %bitcast.104, bf16[2048,768]{1,0:T(8,128)(2,1)} %multiply_convert_fusion.1, f32[768]{0:T(1024)S(1)} %get-tuple-element.2, bf16[4,768,768]{2,1,0:T(8,128)(2,1)} %param.17, pred[2048]{0:T(1024)(128)(4,1)S(1)} %slice_compare_fusion), kind=kOutput, calls=%fused_computation.9 | convolution fusion | flops 2828533760 | bytes 5051392 | tf_op jit(solution)/shard_map/dot_general | solution.py:78
  137.2 0.2 copy.14
  137.4 0.9 copy.15
  (73 shorter events, 0.4 us)
Async XLA Ops:
  7.2 78.1 %copy-start = (s32[128,128,16]{1,2,0:T(8,128)S(1)}, s32[128,128,16]{1,2,0:T(8,128)}, u32[]{:S(2)}) copy-start(s32[128,128,16]{1,2,0:T(8,128)} %param.14) | copy-start | bytes 3145732
  7.2 13.3 %copy-start.1 = (f32[4,32,16,128]{3,2,1,0:T(8,128)S(1)}, f32[4,32,16,128]{3,2,1,0:T(8,128)}, u32[]{:S(2)}) copy-start(f32[4,32,16,128]{3,2,1,0:T(8,128)} %param.10) | copy-start | bytes 3145732
  7.2 107.3 %all-gather.2.cloned.1.call-start = ((), (), s32[]{:S(2)}) async-start(), calls=%async_computation | async-start | bytes 1572864 | tf_op jit(solution)/shard_map/all_gather | solution.py:70
  7.2 14.9 %copy-start.27 = (s32[128]{0:T(128)S(1)}, s32[128]{0:T(128)}, u32[]{:S(2)}) copy-start(s32[128]{0:T(128)} %param.13) | copy-start | bytes 1540
  9.0 15.0 %collective-permute-start = (f32[6,32,1,128]{3,2,1,0:T(1,128)S(1)}, f32[6,32,1,128]{3,2,1,0:T(1,128)S(1)}, u32[]{:S(2)}, u32[]{:S(2)}) collective-permute-start(f32[6,32,1,128]{3,2,1,0:T(1,128)S(1)} %get-tuple-element.12), channel_id=1, source_target_pairs={{0,2},{2,4},{4,6},{6,8},{8,10},{10,12},{12,14},{14,16},{16,18},{18... | collective-permute-start | bytes 294920 | tf_op jit(solution)/shard_map/ppermute | solution.py:18
  9.1 16.4 %copy-start.2 = (f32[32,16,128]{2,1,0:T(8,128)S(1)}, f32[32,16,128]{2,1,0:T(8,128)}, u32[]{:S(2)}) copy-start(f32[32,16,128]{2,1,0:T(8,128)} %param.12) | copy-start | bytes 786436
  9.1 16.4 %copy-start.3 = (f32[32,16,128]{2,1,0:T(8,128)S(1)}, f32[32,16,128]{2,1,0:T(8,128)}, u32[]{:S(2)}) copy-start(f32[32,16,128]{2,1,0:T(8,128)} %param.11) | copy-start | bytes 786436
  9.1 15.6 %collective-permute-start.1 = (f32[6,32,1,128]{3,2,1,0:T(1,128)S(1)}, f32[6,32,1,128]{3,2,1,0:T(1,128)S(1)}, u32[]{:S(2)}, u32[]{:S(2)}) collective-permute-start(f32[6,32,1,128]{3,2,1,0:T(1,128)S(1)} %get-tuple-element.13), channel_id=1, source_target_pairs={{2,0},{4,2},{6,4},{8,6},{10,8},{12,10},{14,12},{16,14},{18,16},{20... | collective-permute-start | bytes 294920 | tf_op jit(solution)/shard_map/ppermute | solution.py:19
  26.4 9.5 %copy-start.4 = (f32[32,16,128]{2,1,0:T(8,128)S(1)}, f32[32,16,128]{2,1,0:T(8,128)}, u32[]{:S(2)}) copy-start(f32[32,16,128]{2,1,0:T(8,128)} %param.11) | copy-start | bytes 786436
  26.4 9.5 %copy-start.9 = (f32[4,32,16,1]{3,2,1,0:T(8,128)S(1)}, f32[4,32,16,1]{3,2,1,0:T(8,128)}, u32[]{:S(2)}) copy-start(f32[4,32,16,1]{3,2,1,0:T(8,128)} %get-tuple-element.30) | copy-start | bytes 24580
  26.4 9.5 %copy-start.10 = (f32[4,32,16,1]{3,2,1,0:T(8,128)S(1)}, f32[4,32,16,1]{3,2,1,0:T(8,128)}, u32[]{:S(2)}) copy-start(f32[4,32,16,1]{3,2,1,0:T(8,128)} %get-tuple-element.31) | copy-start | bytes 24580
  26.4 9.5 %copy-start.11 = (f32[4,32,16,127]{3,2,1,0:T(8,128)S(1)}, f32[4,32,16,127]{3,2,1,0:T(8,128)}, u32[]{:S(2)}) copy-start(f32[4,32,16,127]{3,2,1,0:T(8,128)} %get-tuple-element.32) | copy-start | bytes 3121156
  26.4 9.5 %copy-start.12 = (f32[4,32,16,127]{3,2,1,0:T(8,128)S(1)}, f32[4,32,16,127]{3,2,1,0:T(8,128)}, u32[]{:S(2)}) copy-start(f32[4,32,16,127]{3,2,1,0:T(8,128)} %get-tuple-element.33) | copy-start | bytes 3121156
  26.5 5.0 %collective-permute-start.2 = (f32[5,1,18,128]{3,2,1,0:T(8,128)S(1)}, f32[5,1,18,128]{3,2,1,0:T(8,128)S(1)}, u32[]{:S(2)}, u32[]{:S(2)}) collective-permute-start(f32[5,1,18,128]{3,2,1,0:T(8,128)S(1)} %get-tuple-element.9), channel_id=1, source_target_pairs={{0,1},{2,3},{4,5},{6,7},{8,9},{10,11},{12,13},{14,15},{16,17},{18,... | collective-permute-start | bytes 138248 | tf_op jit(solution)/shard_map/ppermute | solution.py:18
  29.7 6.1 %collective-permute-start.3 = (f32[5,1,18,128]{3,2,1,0:T(8,128)S(1)}, f32[5,1,18,128]{3,2,1,0:T(8,128)S(1)}, u32[]{:S(2)}, u32[]{:S(2)}) collective-permute-start(f32[5,1,18,128]{3,2,1,0:T(8,128)S(1)} %get-tuple-element.8), channel_id=1, source_target_pairs={{1,0},{3,2},{5,4},{7,6},{9,8},{11,10},{13,12},{15,14},{17,16},{19,... | collective-permute-start | bytes 138248 | tf_op jit(solution)/shard_map/ppermute | solution.py:19
  31.2 6.9 %copy-start.15 = (f32[32,16,128]{2,1,0:T(8,128)}, f32[32,16,128]{2,1,0:T(8,128)S(1)}, u32[]{:S(2)}) copy-start(f32[32,16,128]{2,1,0:T(8,128)S(1)} %get-tuple-element.36) | copy-start | bytes 786436
  31.2 6.9 %copy-start.17 = (f32[32,16,128]{2,1,0:T(8,128)}, f32[32,16,128]{2,1,0:T(8,128)S(1)}, u32[]{:S(2)}) copy-start(f32[32,16,128]{2,1,0:T(8,128)S(1)} %get-tuple-element.37) | copy-start | bytes 786436
  31.2 6.9 %copy-start.19 = (f32[32,16,128]{2,1,0:T(8,128)}, f32[32,16,128]{2,1,0:T(8,128)S(1)}, u32[]{:S(2)}) copy-start(f32[32,16,128]{2,1,0:T(8,128)S(1)} %get-tuple-element.38) | copy-start | bytes 786436
  31.2 6.9 %copy-start.21 = (f32[32,16,128]{2,1,0:T(8,128)}, f32[32,16,128]{2,1,0:T(8,128)S(1)}, u32[]{:S(2)}) copy-start(f32[32,16,128]{2,1,0:T(8,128)S(1)} %get-tuple-element.39) | copy-start | bytes 786436
  35.9 2.3 %copy-start.5 = (f32[32,16,128]{2,1,0:T(8,128)}, f32[32,16,128]{2,1,0:T(8,128)S(1)}, u32[]{:S(2)}) copy-start(f32[32,16,128]{2,1,0:T(8,128)S(1)} %get-tuple-element.34) | copy-start | bytes 786436
  35.9 2.3 %copy-start.7 = (f32[32,16,128]{2,1,0:T(8,128)}, f32[32,16,128]{2,1,0:T(8,128)S(1)}, u32[]{:S(2)}) copy-start(f32[32,16,128]{2,1,0:T(8,128)S(1)} %get-tuple-element.35) | copy-start | bytes 786436
  38.3 18.6 %copy-start.6 = (f32[32,16,128]{2,1,0:T(8,128)S(1)}, f32[32,16,128]{2,1,0:T(8,128)}, u32[]{:S(2)}) copy-start(f32[32,16,128]{2,1,0:T(8,128)} %copy-done.5) | copy-start | bytes 786436
  38.3 8.9 %collective-permute-start.4 = (f32[4,32,1,128]{3,2,1,0:T(1,128)S(1)}, f32[4,32,1,128]{3,2,1,0:T(1,128)S(1)}, u32[]{:S(2)}, u32[]{:S(2)}) collective-permute-start(f32[4,32,1,128]{3,2,1,0:T(1,128)S(1)} %get-tuple-element.28), channel_id=1, source_target_pairs={{0,2},{2,4},{4,6},{6,8},{8,10},{10,12},{12,14},{14,16},{16,18},{18... | collective-permute-start | bytes 196616 | tf_op jit(solution)/shard_map/ppermute | solution.py:18
  40.1 8.8 %collective-permute-start.5 = (f32[4,32,1,128]{3,2,1,0:T(1,128)S(1)}, f32[4,32,1,128]{3,2,1,0:T(1,128)S(1)}, u32[]{:S(2)}, u32[]{:S(2)}) collective-permute-start(f32[4,32,1,128]{3,2,1,0:T(1,128)S(1)} %get-tuple-element.29), channel_id=1, source_target_pairs={{2,0},{4,2},{6,4},{8,6},{10,8},{12,10},{14,12},{16,14},{18,16},{20... | collective-permute-start | bytes 196616 | tf_op jit(solution)/shard_map/ppermute | solution.py:19
  49.1 7.8 %copy-start.23 = (f32[4,32,16,1]{3,2,1,0:T(8,128)S(1)}, f32[4,32,16,1]{3,2,1,0:T(8,128)}, u32[]{:S(2)}) copy-start(f32[4,32,16,1]{3,2,1,0:T(8,128)} %get-tuple-element.24) | copy-start | bytes 24580
  49.1 7.8 %copy-start.24 = (f32[4,32,16,1]{3,2,1,0:T(8,128)S(1)}, f32[4,32,16,1]{3,2,1,0:T(8,128)}, u32[]{:S(2)}) copy-start(f32[4,32,16,1]{3,2,1,0:T(8,128)} %get-tuple-element.25) | copy-start | bytes 24580
  49.2 6.3 %collective-permute-start.6 = (f32[4,1,18,128]{3,2,1,0:T(8,128)S(1)}, f32[4,1,18,128]{3,2,1,0:T(8,128)S(1)}, u32[]{:S(2)}, u32[]{:S(2)}) collective-permute-start(f32[4,1,18,128]{3,2,1,0:T(8,128)S(1)} %get-tuple-element.16), channel_id=1, source_target_pairs={{1,0},{3,2},{5,4},{7,6},{9,8},{11,10},{13,12},{15,14},{17,16},{19,... | collective-permute-start | bytes 110600 | tf_op jit(solution)/shard_map/ppermute | solution.py:19
  50.6 6.3 %collective-permute-start.7 = (f32[4,1,18,128]{3,2,1,0:T(8,128)S(1)}, f32[4,1,18,128]{3,2,1,0:T(8,128)S(1)}, u32[]{:S(2)}, u32[]{:S(2)}) collective-permute-start(f32[4,1,18,128]{3,2,1,0:T(8,128)S(1)} %get-tuple-element.17), channel_id=1, source_target_pairs={{0,1},{2,3},{4,5},{6,7},{8,9},{10,11},{12,13},{14,15},{16,17},{18,... | collective-permute-start | bytes 110600 | tf_op jit(solution)/shard_map/ppermute | solution.py:18
  60.7 19.5 %copy-start.8 = (f32[32,16,128]{2,1,0:T(8,128)S(1)}, f32[32,16,128]{2,1,0:T(8,128)}, u32[]{:S(2)}) copy-start(f32[32,16,128]{2,1,0:T(8,128)} %copy-done.7) | copy-start | bytes 786436
  60.7 19.5 %copy-start.16 = (f32[32,16,128]{2,1,0:T(8,128)S(1)}, f32[32,16,128]{2,1,0:T(8,128)}, u32[]{:S(2)}) copy-start(f32[32,16,128]{2,1,0:T(8,128)} %copy-done.15) | copy-start | bytes 786436
  60.8 19.5 %copy-start.18 = (f32[32,16,128]{2,1,0:T(8,128)S(1)}, f32[32,16,128]{2,1,0:T(8,128)}, u32[]{:S(2)}) copy-start(f32[32,16,128]{2,1,0:T(8,128)} %copy-done.17) | copy-start | bytes 786436
  60.8 19.5 %copy-start.20 = (f32[32,16,128]{2,1,0:T(8,128)S(1)}, f32[32,16,128]{2,1,0:T(8,128)}, u32[]{:S(2)}) copy-start(f32[32,16,128]{2,1,0:T(8,128)} %copy-done.19) | copy-start | bytes 786436
  60.8 8.9 %collective-permute-start.8 = (f32[4,32,1,128]{3,2,1,0:T(1,128)S(1)}, f32[4,32,1,128]{3,2,1,0:T(1,128)S(1)}, u32[]{:S(2)}, u32[]{:S(2)}) collective-permute-start(f32[4,32,1,128]{3,2,1,0:T(1,128)S(1)} %get-tuple-element.22), channel_id=1, source_target_pairs={{0,2},{2,4},{4,6},{6,8},{8,10},{10,12},{12,14},{14,16},{16,18},{18... | collective-permute-start | bytes 196616 | tf_op jit(solution)/shard_map/ppermute | solution.py:18
  62.5 9.1 %collective-permute-start.9 = (f32[4,32,1,128]{3,2,1,0:T(1,128)}, f32[4,32,1,128]{3,2,1,0:T(1,128)S(1)}, u32[]{:S(2)}, u32[]{:S(2)}) collective-permute-start(f32[4,32,1,128]{3,2,1,0:T(1,128)} %get-tuple-element.23), channel_id=1, source_target_pairs={{2,0},{4,2},{6,4},{8,6},{10,8},{12,10},{14,12},{16,14},{18,16},{20... | collective-permute-start | bytes 196616 | tf_op jit(solution)/shard_map/ppermute | solution.py:19
  69.6 0.9 copy-start.25
  72.5 7.8 %copy-start.13 = (f32[4,32,16,127]{3,2,1,0:T(8,128)S(1)}, f32[4,32,16,127]{3,2,1,0:T(8,128)}, u32[]{:S(2)}) copy-start(f32[4,32,16,127]{3,2,1,0:T(8,128)} %get-tuple-element.18) | copy-start | bytes 3121156
  72.5 7.8 %copy-start.14 = (f32[4,32,16,127]{3,2,1,0:T(8,128)S(1)}, f32[4,32,16,127]{3,2,1,0:T(8,128)}, u32[]{:S(2)}) copy-start(f32[4,32,16,127]{3,2,1,0:T(8,128)} %get-tuple-element.19) | copy-start | bytes 3121156
  72.5 7.8 %copy-start.22 = (f32[32,16,128]{2,1,0:T(8,128)S(1)}, f32[32,16,128]{2,1,0:T(8,128)}, u32[]{:S(2)}) copy-start(f32[32,16,128]{2,1,0:T(8,128)} %copy-done.21) | copy-start | bytes 786436
  72.5 6.3 %collective-permute-start.10 = (f32[4,1,18,128]{3,2,1,0:T(8,128)S(1)}, f32[4,1,18,128]{3,2,1,0:T(8,128)S(1)}, u32[]{:S(2)}, u32[]{:S(2)}) collective-permute-start(f32[4,1,18,128]{3,2,1,0:T(8,128)S(1)} %get-tuple-element.14), channel_id=1, source_target_pairs={{1,0},{3,2},{5,4},{7,6},{9,8},{11,10},{13,12},{15,14},{17,16},{19,... | collective-permute-start | bytes 110600 | tf_op jit(solution)/shard_map/ppermute | solution.py:19
  74.0 6.3 %collective-permute-start.11 = (f32[4,1,18,128]{3,2,1,0:T(8,128)S(1)}, f32[4,1,18,128]{3,2,1,0:T(8,128)S(1)}, u32[]{:S(2)}, u32[]{:S(2)}) collective-permute-start(f32[4,1,18,128]{3,2,1,0:T(8,128)S(1)} %get-tuple-element.15), channel_id=1, source_target_pairs={{0,1},{2,3},{4,5},{6,7},{8,9},{10,11},{12,13},{14,15},{16,17},{18,... | collective-permute-start | bytes 110600 | tf_op jit(solution)/shard_map/ppermute | solution.py:18
  80.3 13.3 %copy-start.26 = (f32[4,768]{1,0:T(4,128)S(1)}, f32[4,768]{1,0:T(4,128)}, u32[]{:S(2)}) copy-start(f32[4,768]{1,0:T(4,128)} %param.18) | copy-start | bytes 36868
  80.3 34.2 %copy-start.29 = (f32[768]{0:T(1024)S(1)}, f32[768]{0:T(1024)}, u32[]{:S(2)}) copy-start(f32[768]{0:T(1024)} %param.16) | copy-start | bytes 9220
  121.6 9.4 %copy-start.28 = (bf16[768,4,32]{0,2,1:T(8,128)(2,1)S(1)}, bf16[768,4,32]{0,2,1:T(8,128)(2,1)}, u32[]{:S(2)}) copy-start(bf16[768,4,32]{0,2,1:T(8,128)(2,1)} %param.19) | copy-start | bytes 589828
Sparse Core Ops, SparseCore 0:
  85.4 29.0 all-gather.1
where the time goes:
time: 147 us; the launch traced here: 145 us
  starting transfers between devices  38.6 us (26%)
  waiting for transfers between devices  30.2 us (21%)
  local copies, waits for them, and re-layouts  26 us (18%)
  matrix products  22.7 us (15%)
  between operations  15.9 us (11%)
  other arithmetic  11.7 us (8%)
    ppermute x6, starting transfers between devices, padded_2(): after = lax.ppermute(initial, axis, down)  26 us
    all_gather x1, waiting for transfers between devices, first_layer(): lax.all_gather(batch, 'lev', axis=2, tiled=True)  20.8 us
    dot_general x2, matrix products, column_net(): jnp.dot(hidden, w_middle[layer], preferred_element_type=jnp.float32)  16.5 us
    ppermute x6, starting transfers between devices, padded_2(): before = lax.ppermute(last, axis, up)  12.5 us
    scatter x1, local copies, waits for them, and re-layouts, on_device(): active = jnp.zeros((cells + 1,), jnp.int32).at[target].set(1)[:cells]  8.06 us
    slice x4, local copies, waits for them, and re-layouts, advance_region(): jnp.roll(centre, 1, axis=3) - centre  6.84 us
    dot_general x1, matrix products, column_net(): jnp.dot(hidden, w_output.reshape(w_output.shape[0], -1), preferred_elemen...  6.22 us
    ppermute x6, waiting for transfers between devices, padded_2(): after = lax.ppermute(initial, axis, down)  5.76 us
  transfers between devices with their start and end apart: 13, of which 9 were waited for; matrix products, arithmetic and copies ran while one was open for 14% of the time, Pallas kernels for 0%

commit v1 on v0

v1 whole, which is shorter than its diff:
```python
import jax
import jax.numpy as jnp
from jax import lax
from jax.experimental import pallas as pl
from jax.experimental.pallas import tpu as pltpu
from jax.sharding import PartitionSpec as P

CX, CY, HALF, NF = 16, 128, 32, 4
HID, DEPTH = 768, 4
FEAT = NF * HALF
PIECES = (2, 2, 2, 2)
ROWS = 24
OWN = 5
SLOTS = HALF + 10
BLOCK = 4
SIDE = (3 * NF + 3 + 2) * HALF
LEVS = (3 * NF + 2 + 3) * CX
DIAG = 32
VM = pl.BlockSpec(memory_space=pltpu.VMEM)
SM = pl.BlockSpec(memory_space=pltpu.SMEM)
HB = pl.BlockSpec(memory_space=pltpu.HBM)
F32, BF16 = jnp.float32, jnp.bfloat16
PARAMS = pltpu.CompilerParams(vmem_limit_bytes=24 * 1024 * 1024)


def shape(rows, dtype=BF16):
    return jax.ShapeDtypeStruct((rows, CY), dtype)


def side_channels():
    return [(c, d) for c in range(NF + 1) for d in range(3)] + [(NF + 1, 0), (NF + 1, 1)]


def lev_channels():
    return [(c, d) for c in range(NF) for d in range(3)] + [(NF, 0), (NF, 1)] + [(NF + 1, d) for d in range(3)]


DIAG_CELLS = [(0, 0), (1, 0), (0, 1)]


def pack_kernel(fields_hbm, hmix_hbm, vmix_hbm, far, near, up, d_far, d_near, fields, hmix, vmix, sems):
    lev = lax.axis_index("lev")
    odd = lax.axis_index("tile") % 2
    copies = [
        pltpu.make_async_copy(src, dst, sems.at[i])
        for i, (src, dst) in enumerate(((fields_hbm, fields), (hmix_hbm, hmix), (vmix_hbm, vmix)))
    ]
    for copy in copies:
        copy.start()
    for copy in copies:
        copy.wait()
    fields, hmix, vmix = fields.reshape(FEAT * CX, CY), hmix.reshape(HALF * CX, CY), vmix.reshape(HALF * CX, CY)

    def source(c):
        return (fields, c * HALF * CX) if c < NF else ((hmix, 0) if c == NF else (vmix, 0))

    def near_x(d):
        return jnp.where(odd == 0, CX - 1 - d, d)

    def far_x(d):
        return jnp.where(odd == 0, d, CX - 1 - d)

    for k, (c, d) in enumerate(side_channels()):
        ref, base = source(c)
        rows = pl.ds(k * HALF, HALF)
        far[rows, :] = ref[pl.ds(base + far_x(d), HALF, stride=CX), :].astype(BF16)
        near[rows, :] = ref[pl.ds(base + near_x(d), HALF, stride=CX), :].astype(BF16)
    for k, (c, d) in enumerate(lev_channels()):
        ref, base = source(c)
        at = jnp.where(lev == 0, HALF - 1 - d, d) * CX + base
        up[pl.ds(k * CX, CX), :] = ref[pl.ds(pl.multiple_of(at, CX), CX), :].astype(BF16)
    for out, place in ((d_far, far_x), (d_near, near_x)):
        cells = []
        for c in range(NF + 2):
            ref, base = source(c)
            for dx, dl in DIAG_CELLS:
                at = jnp.where(lev == 0, HALF - 1 - dl, dl) * CX + base
                cells.append(ref[pl.ds(at + place(dx), 1), :])
        cells.append(jnp.zeros((DIAG - len(cells), CY), F32))
        out[...] = jnp.concatenate(cells, axis=0).astype(BF16)


def dynamics_kernel(flags, fields_hbm, hmix_hbm, vmix_hbm, from_far, from_near, from_lev, d_far, d_near, *rest):
    count = len(PIECES)
    outs, scratch = rest[: 1 + 2 * count], rest[1 + 2 * count :]
    advanced, own, other = outs[0], outs[1 : 1 + count], outs[1 + count :]
    s0, s1, s2, hv, coef, sems = scratch
    lev = flags[2]
    odd = flags[4]
    copies = []
    for c in range(NF):
        copies.append((fields_hbm.at[c], s0.at[c, OWN : OWN + HALF, 0:CX]))
    copies.append((hmix_hbm, hv.at[0, OWN : OWN + HALF, 0:CX]))
    copies.append((vmix_hbm, hv.at[1, OWN : OWN + HALF, 0:CX]))
    copies = [pltpu.make_async_copy(src, dst, sems.at[i]) for i, (src, dst) in enumerate(copies)]
    for copy in copies:
        copy.start()

    s0 = s0.reshape(NF * SLOTS * ROWS, CY)
    hv = hv.reshape(2 * SLOTS * ROWS, CY)

    def place(c, slot):
        ref, k = (s0, c) if c < NF else (hv, c - NF)
        return ref, (k * SLOTS + slot) * ROWS

    zero = jnp.zeros((ROWS, CY), F32)
    ghost = jnp.where(lev == 0, OWN - 1, OWN + HALF)

    def still(ref):
        for f in range(NF):
            ref[pl.ds(pl.multiple_of((f * SLOTS + ghost) * ROWS, 8), ROWS), :] = zero

    still(s0)
    hv[pl.ds(pl.multiple_of((SLOTS + ghost) * ROWS, 8), ROWS), :] = zero

    row = lax.broadcasted_iota(jnp.int32, (CY, CY), 0)
    col = lax.broadcasted_iota(jnp.int32, (CY, CY), 1)

    def turned(flag, value):
        turn = jnp.where(jnp.where(flag > 0, CY - 1 - row, row) == col, 1.0, 0.0).astype(BF16)
        return jnp.dot(value, turn, preferred_element_type=F32)

    def near_row(d):
        return jnp.where(odd == 0, CX + d, ROWS - 1 - d)

    def far_row(d):
        return jnp.where(odd == 0, ROWS - 1 - d, CX + d)

    def beyond(d):
        return jnp.where(lev == 0, OWN + HALF + d, OWN - 1 - d)

    for flag, sides, corners, at_row in ((flags[0], from_near, d_near, near_row), (flags[1], from_far, d_far, far_row)):
        sides = turned(flag, sides[...])
        corners = turned(flag, corners[...])
        for k, (c, d) in enumerate(side_channels()):
            ref, base = place(c, OWN)
            ref[pl.ds(base + at_row(d), HALF, stride=ROWS), :] = sides[k * HALF : (k + 1) * HALF]
        for c in range(NF + 2):
            for n, (dx, dl) in enumerate(DIAG_CELLS):
                ref, base = place(c, beyond(dl))
                k = c * len(DIAG_CELLS) + n
                ref[pl.ds(base + at_row(dx), 1), :] = corners[k : k + 1]
    for k, (c, d) in enumerate(lev_channels()):
        ref, base = place(c, beyond(d))
        ref[pl.ds(pl.multiple_of(base, 8), CX), :] = from_lev[pl.ds(k * CX, CX), :].astype(F32)
    for copy in copies:
        copy.wait()

    def load(ref, k, slot, levels, rows=ROWS):
        at = pl.multiple_of((k * SLOTS + slot) * ROWS, 8)
        return ref[pl.ds(at, levels * ROWS), :].reshape(levels, ROWS, CY)[:, :rows]

    def save(ref, k, slot, value):
        levels = value.shape[0]
        at = pl.multiple_of((k * SLOTS + slot) * ROWS, 8)
        ref[pl.ds(at, levels * ROWS), :] = value.reshape(levels * ROWS, CY)

    def coefficients(at):
        h = 0.5 * load(hv, 0, at, BLOCK)
        v = 0.5 * load(hv, 1, at - 1, BLOCK + 2)
        pairs = v[1:] + v[:-1]
        upper, lower = pairs[1:], pairs[:-1]
        c_east = h + pltpu.roll(h, ROWS - 1, 1)
        c_west = h + pltpu.roll(h, 1, 1)
        c_north = h + pltpu.roll(h, CY - 1, 2)
        c_south = h + pltpu.roll(h, 1, 2)
        centre = 1.0 - (((c_east + c_west) + (c_north + c_south)) + (upper + lower))
        k = (c_east, c_west, c_north, c_south, upper, lower, centre)
        for n, value in enumerate(k):
            save(coef, n, at, value)
        return k

    def substep(source, k, at, rows, store):
        for f in range(NF):
            column = load(source, f, at - 1, BLOCK + 2)
            cell, centre = column[1:-1], column[1:-1, :rows]
            value = k[6] * centre
            value += k[0] * pltpu.roll(cell, ROWS - 1, 1)[:, :rows]
            value += k[1] * pltpu.roll(cell, 1, 1)[:, :rows]
            value += k[2] * pltpu.roll(centre, CY - 1, 2)
            value += k[3] * pltpu.roll(centre, 1, 2)
            value += k[4] * column[2:, :rows]
            value += k[5] * column[:-2, :rows]
            store(f, at, value)

    def kept(at, rows):
        return [load(coef, n, at, BLOCK, rows) for n in range(7)]

    def into(target):
        return lambda f, at, value: save(target, f, at, value)

    def final(f, at, value):
        advanced[pl.ds(pl.multiple_of((f * HALF + at - OWN) * CX, CX), BLOCK * CX), :] = value.reshape(BLOCK * CX, CY)

    def one(i):
        at = OWN - 2 + i * BLOCK
        substep(s0, coefficients(at), at, ROWS, into(s1))

    def two(i):
        at = OWN - 3 + (i - 1) * BLOCK
        substep(s1, kept(at, ROWS), at, ROWS, into(s2))

    def three(i):
        at = OWN + (i - 3) * BLOCK
        substep(s2, kept(at, CX), at, CX, final)

    def sweep(i, parts):
        for part in parts:
            part(i)
        still(s1)
        still(s2)

    last = HALF // BLOCK
    sweep(0, (one,))
    for i in (1, 2):
        sweep(i, (two, one))

    for i in range(3, last + 1):
        sweep(i, (three, two, one))
    sweep(last + 1, (three, two))
    sweep(last + 2, (three,))

    x = 0
    for piece, width in enumerate(PIECES):
        for i in range(width):
            low = advanced[pl.ds(x, FEAT, stride=CX), :].astype(BF16)
            high = advanced[pl.ds(x + CX // 2, FEAT, stride=CX), :].astype(BF16)
            rows = pl.ds(i * FEAT, FEAT)
            own[piece][rows, :] = jnp.where(lev == 0, low, high)
            other[piece][rows, :] = jnp.where(lev == 0, high, low)
            x += 1


def prepare_kernel(
    early, edge_flip, batch_slots, w_first, w_mid, b_first, b_mid,
    flags, w_first_out, w_mid_out, b_first_out, b_mid_out, flips, slots, sems,
):
    place = lax.axis_index("tile")
    odd = place % 2
    count = edge_flip.shape[0]
    pairs = (
        (edge_flip, flips),
        (batch_slots.at[place, 0:8], slots),
        (w_mid, w_mid_out),
        (w_first, w_first_out),
    )
    copies = [pltpu.make_async_copy(src, dst, sems.at[i]) for i, (src, dst) in enumerate(pairs)]
    for copy in copies:
        copy.start()
    b_first_out[...] = jnp.broadcast_to(b_first[...], (CY, HID)).T
    for k in range(DEPTH):
        b_mid_out[pl.ds(k * HID, HID), :] = jnp.broadcast_to(b_mid[k : k + 1, :], (CY, HID)).T
    for copy in copies:
        copy.wait()
    east = flips[(place + 1) % count]
    west = flips[place]
    flags[0] = jnp.where(odd == 0, east, west)
    flags[1] = jnp.where(odd == 0, west, east)
    flags[2] = lax.axis_index("lev")
    flags[3] = jnp.where(slots[0, 0] >= 0, 1, 0)
    flags[4] = odd


def silu(z):
    half = 0.5 * z
    return half + half * jnp.tanh(half)


def net_kernel(flags, own, other, w_first, b_first, w_mid, b_mid, wo_own, wo_other, out_own, out_other, ha, hb):
    n = own.shape[0] // FEAT
    lev = flags[2]
    tile = 256

    @pl.when(flags[3] > 0)
    def _():
        def flat(ref):
            return jnp.concatenate([ref[pl.ds(i * FEAT, FEAT), :] for i in range(n)], axis=1)

        def first_rows(block):
            return [w_first[pl.ds(pl.multiple_of(f * 2 * HALF + block * HALF, HALF), HALF), :] for f in range(NF)]

        def layer(weights, bias, start, value, target):
            for m in range(0, HID, tile):
                part = lax.dot_general(weights(m), value, (((0,), (0,)), ((), ())), preferred_element_type=F32)
                shift = bias[pl.ds(start + m, tile), :]
                target[pl.ds(m, tile), :] = silu(part + jnp.concatenate([shift] * n, axis=1)).astype(BF16)

        w0 = jnp.concatenate(first_rows(lev) + first_rows(1 - lev), axis=0)
        layer(lambda m: w0[:, m : m + tile], b_first, 0, jnp.concatenate([flat(own), flat(other)], axis=0), ha)
        source, target = ha, hb
        for k in range(DEPTH):
            layer(lambda m: w_mid[pl.ds(k * HID, HID), m : m + tile], b_mid, k * HID, source[...], target)
            source, target = target, source
        hidden = source[...]
        for w, out in ((wo_other, out_other), (wo_own, out_own)):
            result = jnp.dot(w[...], hidden, preferred_element_type=F32).astype(BF16)
            for i in range(n):
                out[pl.ds(i * FEAT, FEAT), :] = result[:, i * CY : (i + 1) * CY]


def finish_kernel(flags, *rest):
    count = len(PIECES)
    mine, theirs = rest[:count], rest[count : 2 * count]
    tendency, wide = rest[2 * count :]
    lev = flags[2]
    active = flags[3] > 0

    @pl.when(active)
    def _():
        x = 0
        for piece, width in enumerate(PIECES):
            for i in range(width):
                rows = pl.ds(i * FEAT, FEAT)
                a, b = mine[piece][rows, :], theirs[piece][rows, :]
                wide[pl.ds(x, FEAT, stride=CX), :] = jnp.where(lev == 0, a, b).astype(F32)
                wide[pl.ds(x + CX // 2, FEAT, stride=CX), :] = jnp.where(lev == 0, b, a).astype(F32)
                x += 1
        tendency[...] = wide[...].astype(BF16)

    @pl.when(jnp.logical_not(active))
    def _():
        tendency[...] = jnp.zeros(tendency.shape, BF16)


def along_lev(value):
    return lax.ppermute(value, "lev", [(0, 1), (1, 0)])


def across(value, first, turn):
    count = lax.axis_size("tile")
    pairs = []
    for i in range(first, count, 2):
        for k in range(2):
            a, b = 2 * i + k, 2 * ((i + 1) % count) + (1 - k if turn else k)
            pairs += [(a, b), (b, a)]
    return lax.ppermute(value, ("tile", "lev"), sorted(pairs))


def on_device(
    fields, horizontal_mix, vertical_mix, edge_flip, batch_slots,
    w_first, bias_first, w_middle, bias_middle, w_output,
):
    fields_hbm, hmix_hbm, vmix_hbm = (
        pltpu.with_memory_space_constraint(value, pltpu.HBM) for value in (fields, horizontal_mix, vertical_mix)
    )
    far, near, up, d_far, d_near = pl.pallas_call(
        pack_kernel,
        in_specs=[HB] * 3,
        out_specs=[VM] * 5,
        out_shape=[shape(SIDE), shape(SIDE), shape(LEVS), shape(DIAG), shape(DIAG)],
        scratch_shapes=[
            pltpu.VMEM((NF, HALF, CX, CY), F32),
            pltpu.VMEM((HALF, CX, CY), F32),
            pltpu.VMEM((HALF, CX, CY), F32),
            pltpu.SemaphoreType.DMA((3,)),
        ],
        compiler_params=PARAMS,
    )(fields_hbm, hmix_hbm, vmix_hbm)
    from_far = across(far, 1, False)
    from_lev = along_lev(up)
    from_near = across(near, 0, False)
    from_d_near = across(d_near, 0, True)
    from_d_far = across(d_far, 1, True)

    def in_hbm(value):
        return pltpu.with_memory_space_constraint(value, pltpu.HBM)

    flags, w_first_v, w_mid_v, b_first, b_mid = pl.pallas_call(
        prepare_kernel,
        in_specs=[HB] * 5 + [VM, VM],
        out_specs=[SM] + [VM] * 4,
        out_shape=[
            jax.ShapeDtypeStruct((5,), jnp.int32),
            pltpu.VMEM((2 * FEAT, HID), BF16),
            pltpu.VMEM((DEPTH * HID, HID), BF16),
            pltpu.VMEM((HID, CY), F32),
            pltpu.VMEM((DEPTH * HID, CY), F32),
        ],
        scratch_shapes=[
            pltpu.SMEM(edge_flip.shape, jnp.int32),
            pltpu.SMEM((8, batch_slots.shape[1]), jnp.int32),
            pltpu.SemaphoreType.DMA((4,)),
        ],
        compiler_params=PARAMS,
    )(
        in_hbm(d_near),
        in_hbm(edge_flip),
        in_hbm(batch_slots.transpose(0, 2, 1)),
        in_hbm(w_first.reshape(2 * FEAT, HID)),
        in_hbm(w_middle.reshape(DEPTH * HID, HID)),
        bias_first.reshape(1, HID),
        bias_middle,
    )
    wo_own = w_output.reshape(HID, FEAT).T
    flags, wo_own, from_far, from_lev, from_near, from_d_near, from_d_far = lax.optimization_barrier(
        (flags, wo_own, from_far, from_lev, from_near, from_d_near, from_d_far)
    )
    wo_other = along_lev(wo_own)

    outs = pl.pallas_call(
        dynamics_kernel,
        in_specs=[SM] + [HB] * 3 + [VM] * 5,
        out_specs=[VM] * (1 + 2 * len(PIECES)),
        out_shape=[shape(FEAT * CX, F32)] + [shape(n * FEAT) for n in PIECES] * 2,
        scratch_shapes=[
            pltpu.VMEM((NF, SLOTS, ROWS, CY), F32),
            pltpu.VMEM((NF * SLOTS * ROWS, CY), F32),
            pltpu.VMEM((NF * SLOTS * ROWS, CY), F32),
            pltpu.VMEM((2, SLOTS, ROWS, CY), F32),
            pltpu.VMEM((7 * SLOTS * ROWS, CY), F32),
            pltpu.SemaphoreType.DMA((NF + 2,)),
        ],
        compiler_params=PARAMS,
    )(flags, fields_hbm, hmix_hbm, vmix_hbm, from_far, from_near, from_lev, from_d_far, from_d_near)
    advanced, own, other = outs[0], outs[1 : 1 + len(PIECES)], outs[1 + len(PIECES) :]

    received = [along_lev(piece) for piece in other]
    mine, theirs = [], []
    for k, width in enumerate(PIECES):
        rows = width * FEAT
        a, b = pl.pallas_call(
            net_kernel,
            in_specs=[SM] + [VM] * 8,
            out_specs=[VM] * 2,
            out_shape=[shape(rows)] * 2,
            scratch_shapes=[pltpu.VMEM((HID, width * CY), BF16)] * 2,
            compiler_params=PARAMS,
        )(
            flags, own[k], received[k], w_first_v, b_first, w_mid_v, b_mid, wo_own, wo_other
        )
        mine.append(a)
        theirs.append(along_lev(b))
    tendency = pl.pallas_call(
        finish_kernel,
        in_specs=[SM] + [VM] * (2 * len(PIECES)),
        out_specs=VM,
        out_shape=shape(FEAT * CX),
        scratch_shapes=[pltpu.VMEM((FEAT * CX, CY), F32)],
        compiler_params=PARAMS,
    )(flags, *mine, *theirs)
    whole = (NF, HALF, CX, CY)
    return advanced.reshape(whole), tendency.reshape(whole)


def solution(mesh):
    return jax.shard_map(
        on_device,
        mesh=mesh,
        in_specs=(
            P(None, "lev", "tile", None),
            P("lev", "tile", None),
            P("lev", "tile", None),
            P(),
            P(),
            P(),
            P(),
            P(),
            P(),
            P(None, None, "lev"),
        ),
        out_specs=(P(None, "lev", "tile", None), P(None, "lev", "tile", None)),
        check_vma=False,
    )
```

time: 147 us -> 55.2 us (0.38); the launches traced: 145 us -> 54.9 us
  Pallas kernels: 0 us -> 25.6 us
  waiting for transfers between devices: 30.2 us -> 5.27 us
  local copies, waits for them, and re-layouts: 26 us -> 1.41 us
  matrix products: 22.7 us -> 0 us
  starting transfers between devices: 38.6 us -> 21.9 us
  between operations: 15.9 us -> 0.75 us
  other arithmetic: 11.7 us -> 0 us
    pallas_call x0 -> x8, Pallas kernels: none -> 25.6 us  [the longest x4 12 us: on_device(): pl.pallas_call(net_kernel, in_specs=[SM] + [VM] * 8, out_specs=[VM] * 2,...]
    dot_general x3 -> x0, matrix products: 22.7 us -> none  [the longest x2 16.5 us: column_net(): jnp.dot(hidden, w_middle[layer], preferred_element_type=jnp.float32)]
    all_gather x1 -> x0, waiting for transfers between devices: 20.8 us -> none  [first_layer(): lax.all_gather(batch, 'lev', axis=2, tiled=True)]
    ppermute x12 -> x14, starting transfers between devices: 38.6 us -> 21.9 us  [the longest x10 12.6 us: along_lev(): return lax.ppermute(value, 'lev', [(0, 1), (1, 0)])]
    slice x12 -> x0, local copies, waits for them, and re-layouts: 10.1 us -> none  [the longest x4 6.84 us: advance_region(): jnp.roll(centre, 1, axis=3) - centre]
    scatter x1 -> x0, local copies, waits for them, and re-layouts: 8.06 us -> none  [on_device(): active = jnp.zeros((cells + 1,), jnp.int32).at[target].set(1)[:cells]]
    add x2 -> x0, other arithmetic: 5.34 us -> none  [advance_region(): return centre + change]
    ppermute x12 -> x14, waiting for transfers between devices: 9.37 us -> 5.27 us  [the longest x10 3.11 us: along_lev(): return lax.ppermute(value, 'lev', [(0, 1), (1, 0)])]
  transfers between devices with their start and end apart: 13 -> 14, of which waited for: 9 -> 3; matrix products, arithmetic and copies ran while one was open for 14% -> 1% of each run, Pallas kernels for 0% -> 40%
where the time goes in v1:
time: 55.2 us; the launch traced here: 54.9 us
  Pallas kernels  25.6 us (46%)
  starting transfers between devices  21.9 us (40%)
  waiting for transfers between devices  5.27 us (10%)
  local copies, waits for them, and re-layouts  1.41 us (3%)
  between operations  0.75 us (1%)
    ppermute x10, starting transfers between devices, along_lev(): return lax.ppermute(value, 'lev', [(0, 1), (1, 0)])  12.6 us
    pallas_call x4, Pallas kernels, on_device(): pl.pallas_call(net_kernel, in_specs=[SM] + [VM] * 8, out_specs=[VM] * 2,...  12 us
    ppermute x4, starting transfers between devices, across(): return lax.ppermute(value, ('tile', 'lev'), sorted(pairs))  9.31 us
    pallas_call x1, Pallas kernels, on_device(): pl.pallas_call(dynamics_kernel, in_specs=[SM] + [HB] * 3 + [VM] * 5, out_...  6.46 us
    pallas_call x1, Pallas kernels, on_device(): pl.pallas_call(prepare_kernel, in_specs=[HB] * 5 + [VM, VM], out_specs=[S...  3.46 us
    ppermute x10, waiting for transfers between devices, along_lev(): return lax.ppermute(value, 'lev', [(0, 1), (1, 0)])  3.11 us
    ppermute x4, waiting for transfers between devices, across(): return lax.ppermute(value, ('tile', 'lev'), sorted(pairs))  2.16 us
    pallas_call x1, Pallas kernels, on_device(): pl.pallas_call(finish_kernel, in_specs=[SM] + [VM] * (2 * len(PIECES)), o...  1.94 us
  transfers between devices with their start and end apart: 14, of which 3 were waited for; matrix products, arithmetic and copies ran while one was open for 1% of the time, Pallas kernels for 40%

profile of v1, /device:TPU:24, one launch (start us, length us, event | category | flops | bytes accessed | tf_op | source)
XLA Modules:
  0.0 54.9 jit_solution(2684047479305929900)
XLA Ops:
  0.6 0.0 copy-start
  0.6 1.7 %shard_map.113 = (bf16[544,128]{1,0:T(8,128)(2,1)S(1)}, bf16[544,128]{1,0:T(8,128)(2,1)S(1)}, bf16[272,128]{1,0:T(8,128)(2,1)S(1)}, bf16[32,128]{1,0:T(8,128)(2,1)S(1)}, bf16[32,128]{1,0:T(8,128)(2,1)S(1)}) custom-call(f32[4,32,16,128]{3,2,1,0:T(8,128)} %fields_hbm.3, f32[32,16,128]{2,1,0:T(8,128)} %hmix_hbm.3, f32[32,16,128]{2,1,0:T(8,128)} %vmix_hbm.3), custom_call_target="tpu_custom_call" | custom-call | tf_op jit(solution)/shard_map/pallas_call | solution.py:346
  2.4 0.0 copy-start.2
  2.4 8.2 %collective-permute-start = (bf16[544,128]{1,0:T(8,128)(2,1)S(1)}, bf16[544,128]{1,0:T(8,128)(2,1)S(1)}, u32[]{:S(2)}, u32[]{:S(2)}) collective-permute-start(bf16[544,128]{1,0:T(8,128)(2,1)S(1)} %get-tuple-element.38), channel_id=1, source_target_pairs={{0,254},{1,255},{2,4},{3,5},{4,2},{5,3},{6,8},{7,9},{8,6},{9,7},{1... | collective-permute-start | bytes 417800 | tf_op jit(solution)/shard_map/ppermute | solution.py:336
  10.6 0.0 collective-permute-start.2
  10.6 1.0 %collective-permute-start.1 = (bf16[272,128]{1,0:T(8,128)(2,1)S(1)}, bf16[272,128]{1,0:T(8,128)(2,1)S(1)}, u32[]{:S(2)}, u32[]{:S(2)}) collective-permute-start(bf16[272,128]{1,0:T(8,128)(2,1)S(1)} %get-tuple-element.39), channel_id=1, source_target_pairs={{0,1},{1,0},{2,3},{3,2},{4,5},{5,4},{6,7},{7,6},{8,9},{9,8},{10,11... | collective-permute-start | bytes 208904 | tf_op jit(solution)/shard_map/ppermute | solution.py:326
  11.6 0.8 %collective-permute-start.3 = (bf16[32,128]{1,0:T(8,128)(2,1)S(1)}, bf16[32,128]{1,0:T(8,128)(2,1)S(1)}, u32[]{:S(2)}, u32[]{:S(2)}) collective-permute-start(bf16[32,128]{1,0:T(8,128)(2,1)S(1)} %get-tuple-element.36.early), channel_id=1, source_target_pairs={{0,3},{1,2},{2,1},{3,0},{4,7},{5,6},{6,5},{7,4},{8,11},{9,10},{10,... | collective-permute-start | bytes 24584 | tf_op jit(solution)/shard_map/ppermute | solution.py:336
  12.5 0.3 collective-permute-start.4
  12.7 0.7 %reshape.24.b_first = f32[1,768]{1,0:T(1,128)S(1)} reshape(f32[768]{0:T(1024)} %param.16) | data formatting | bytes 6144 | tf_op jit(solution)/shard_map/reshape | solution.py:391
  13.4 0.0 copy-done.2
  13.4 0.0 copy-start.1
  13.4 0.7 %copy-done.1 = f32[4,768]{1,0:T(4,128)S(1)} copy-done((f32[4,768]{1,0:T(4,128)S(1)}, f32[4,768]{1,0:T(4,128)}, u32[]{:S(2)}) %copy-start.1) | copy-done | bytes 12312
  14.1 3.5 %shard_map.114 = (s32[5]{0:T(128)S(1)}, bf16[256,768]{1,0:T(8,128)(2,1)S(1)}, bf16[3072,768]{1,0:T(8,128)(2,1)S(1)}, f32[768,128]{1,0:T(8,128)S(1)}, f32[3072,128]{1,0:T(8,128)S(1)}) custom-call(bf16[32,128]{1,0:T(8,128)(2,1)} %copy-done.2, s32[128]{0:T(128)} %edge_flip.1, s32[128,16,128]{2,1,0:T(8,128)} %bitcast.14, bf16[256,768]{1,0:T(8,128)(2,1)} %bitcast.16, ...), custom_call_target="tpu_custom_call" | custom-call | tf_op jit(solution)/shard_map/pallas_call | solution.py:368
  17.6 0.0 collective-permute-done.3.d_near
  17.6 2.1 %collective-permute-done.4.d_far = bf16[32,128]{1,0:T(8,128)(2,1)S(1)} collective-permute-done((bf16[32,128]{1,0:T(8,128)(2,1)S(1)}, bf16[32,128]{1,0:T(8,128)(2,1)S(1)}, u32[]{:S(2)}, u32[]{:S(2)}) %collective-permute-start.4) | collective-permute-done | bytes 8224 | tf_op jit(solution)/shard_map/ppermute | solution.py:336
  19.8 0.0 collective-permute-done.1.from_lev
  19.8 0.0 collective-permute-done.from_far
  19.8 0.0 collective-permute-done.2.from_near
  19.8 0.0 copy-done
  19.8 3.0 %collective-permute-start.6 = (bf16[128,768]{1,0:T(8,128)(2,1)S(1)}, bf16[128,768]{1,0:T(8,128)(2,1)S(1)}, u32[]{:S(2)}, u32[]{:S(2)}) collective-permute-start(bf16[128,768]{1,0:T(8,128)(2,1)S(1)} %bitcast.8), channel_id=1, source_target_pairs={{0,1},{1,0},{2,3},{3,2},{4,5},{5,4},{6,7},{7,6},{8,9},{9,8},{10,11... | collective-permute-start | bytes 589832 | tf_op jit(solution)/shard_map/ppermute | solution.py:326
  22.8 6.5 %shard_map.115 = (f32[2048,128]{1,0:T(8,128)}, bf16[256,128]{1,0:T(8,128)(2,1)S(1)}, bf16[256,128]{1,0:T(8,128)(2,1)S(1)}, bf16[256,128]{1,0:T(8,128)(2,1)S(1)},...) custom-call(s32[5]{0:T(128)S(1)} %get-tuple-element.42.flags, ...), custom_call_target="tpu_custom_call" | custom-call | tf_op jit(solution)/shard_map/pallas_call | solution.py:400
  29.3 0.1 collective-permute-start.9
  29.4 2.0 %collective-permute-start.8 = (bf16[256,128]{1,0:T(8,128)(2,1)S(1)}, bf16[256,128]{1,0:T(8,128)(2,1)S(1)}, u32[]{:S(2)}, u32[]{:S(2)}) collective-permute-start(bf16[256,128]{1,0:T(8,128)(2,1)S(1)} %get-tuple-element.61), channel_id=1, source_target_pairs={{0,1},{1,0},{2,3},{3,2},{4,5},{5,4},{6,7},{7,6},{8,9},{9,8},{10,11... | collective-permute-start | bytes 196616 | tf_op jit(solution)/shard_map/ppermute | solution.py:326
  31.4 0.1 collective-permute-start.7
  31.5 2.0 %collective-permute-start.5 = (bf16[256,128]{1,0:T(8,128)(2,1)S(1)}, bf16[256,128]{1,0:T(8,128)(2,1)S(1)}, u32[]{:S(2)}, u32[]{:S(2)}) collective-permute-start(bf16[256,128]{1,0:T(8,128)(2,1)S(1)} %get-tuple-element.50), channel_id=1, source_target_pairs={{0,1},{1,0},{2,3},{3,2},{4,5},{5,4},{6,7},{7,6},{8,9},{9,8},{10,11... | collective-permute-start | bytes 196616 | tf_op jit(solution)/shard_map/ppermute | solution.py:326
  33.4 0.8 %collective-permute-done.9.other = bf16[256,128]{1,0:T(8,128)(2,1)S(1)} collective-permute-done((bf16[256,128]{1,0:T(8,128)(2,1)S(1)}, bf16[256,128]{1,0:T(8,128)(2,1)S(1)}, u32[]{:S(2)}, u32[]{:S(2)}) %collective-permute-start.9) | collective-permute-done | bytes 65568 | tf_op jit(solution)/shard_map/ppermute | solution.py:326
  34.2 0.0 collective-permute-done.6.wo_other
  34.2 3.1 %shard_map.119 = (bf16[256,128]{1,0:T(8,128)(2,1)S(1)}, bf16[256,128]{1,0:T(8,128)(2,1)S(1)}) custom-call(s32[5]{0:T(128)S(1)} %get-tuple-element.42.flags, bf16[256,128]{1,0:T(8,128)(2,1)S(1)} %get-tuple-element.63.own, bf16[256,128]{1,0:T(8,128)(2,1)S(1)} %collective-permute-done.9.other, bf16[256,768]{1,0:T(8,128)(2,1)S(1)} %get-tuple-element.51.w_first, ...), custom_call_target="tpu_custom_call" | custom-call | tf_op jit(solution)/shard_map/pallas_call | solution.py:421
  37.4 0.1 collective-permute-start.13
  37.5 0.0 collective-permute-done.8.other
  37.5 3.0 %shard_map.118 = (bf16[256,128]{1,0:T(8,128)(2,1)S(1)}, bf16[256,128]{1,0:T(8,128)(2,1)S(1)}) custom-call(s32[5]{0:T(128)S(1)} %get-tuple-element.42.flags, bf16[256,128]{1,0:T(8,128)(2,1)S(1)} %get-tuple-element.60.own, bf16[256,128]{1,0:T(8,128)(2,1)S(1)} %collective-permute-done.8.other, bf16[256,768]{1,0:T(8,128)(2,1)S(1)} %get-tuple-element.51.w_first, ...), custom_call_target="tpu_custom_call" | custom-call | tf_op jit(solution)/shard_map/pallas_call | solution.py:421
  40.5 2.1 %collective-permute-start.12 = (bf16[256,128]{1,0:T(8,128)(2,1)S(1)}, bf16[256,128]{1,0:T(8,128)(2,1)S(1)}, u32[]{:S(2)}, u32[]{:S(2)}) collective-permute-start(bf16[256,128]{1,0:T(8,128)(2,1)S(1)} %get-tuple-element.68), channel_id=1, source_target_pairs={{0,1},{1,0},{2,3},{3,2},{4,5},{5,4},{6,7},{7,6},{8,9},{9,8},{10,11... | collective-permute-start | bytes 196616 | tf_op jit(solution)/shard_map/ppermute | solution.py:326
  42.6 0.0 collective-permute-done.7.other
  42.6 3.0 %shard_map.117 = (bf16[256,128]{1,0:T(8,128)(2,1)S(1)}, bf16[256,128]{1,0:T(8,128)(2,1)S(1)}) custom-call(s32[5]{0:T(128)S(1)} %get-tuple-element.42.flags, bf16[256,128]{1,0:T(8,128)(2,1)S(1)} %get-tuple-element.57.own, bf16[256,128]{1,0:T(8,128)(2,1)S(1)} %collective-permute-done.7.other, bf16[256,768]{1,0:T(8,128)(2,1)S(1)} %get-tuple-element.51.w_first, ...), custom_call_target="tpu_custom_call" | custom-call | tf_op jit(solution)/shard_map/pallas_call | solution.py:421
  45.5 0.1 collective-permute-start.11
  45.6 0.0 collective-permute-done.5.other
  45.6 3.0 %shard_map.116 = (bf16[256,128]{1,0:T(8,128)(2,1)S(1)}, bf16[256,128]{1,0:T(8,128)(2,1)S(1)}) custom-call(s32[5]{0:T(128)S(1)} %get-tuple-element.42.flags, bf16[256,128]{1,0:T(8,128)(2,1)S(1)} %get-tuple-element.49.own, bf16[256,128]{1,0:T(8,128)(2,1)S(1)} %collective-permute-done.5.other, bf16[256,768]{1,0:T(8,128)(2,1)S(1)} %get-tuple-element.51.w_first, ...), custom_call_target="tpu_custom_call" | custom-call | tf_op jit(solution)/shard_map/pallas_call | solution.py:421
  48.6 2.1 %collective-permute-start.10 = (bf16[256,128]{1,0:T(8,128)(2,1)S(1)}, bf16[256,128]{1,0:T(8,128)(2,1)S(1)}, u32[]{:S(2)}, u32[]{:S(2)}) collective-permute-start(bf16[256,128]{1,0:T(8,128)(2,1)S(1)} %get-tuple-element.66), channel_id=1, source_target_pairs={{0,1},{1,0},{2,3},{3,2},{4,5},{5,4},{6,7},{7,6},{8,9},{9,8},{10,11... | collective-permute-start | bytes 196616 | tf_op jit(solution)/shard_map/ppermute | solution.py:326
  50.7 0.0 collective-permute-done.13.rest_7_
  50.7 0.0 collective-permute-done.12.rest_6_
  50.7 0.0 collective-permute-done.11.rest_5_
  50.7 2.3 %collective-permute-done.10.rest_4_ = bf16[256,128]{1,0:T(8,128)(2,1)S(1)} collective-permute-done((bf16[256,128]{1,0:T(8,128)(2,1)S(1)}, bf16[256,128]{1,0:T(8,128)(2,1)S(1)}, u32[]{:S(2)}, u32[]{:S(2)}) %collective-permute-start.10) | collective-permute-done | bytes 65568 | tf_op jit(solution)/shard_map/ppermute | solution.py:326
  53.0 1.9 %shard_map.120 = bf16[2048,128]{1,0:T(8,128)(2,1)} custom-call(s32[5]{0:T(128)S(1)} %get-tuple-element.42.flags, bf16[256,128]{1,0:T(8,128)(2,1)S(1)} %get-tuple-element.56.rest_0_, bf16[256,128]{1,0:T(8,128)(2,1)S(1)} %get-tuple-element.59.rest_1_, bf16[256,128]{1,0:T(8,128)(2,1)S(1)} %get-tuple-element.62.rest_2_, ...), custom_call_target="tpu_custom_call" | custom-call | tf_op jit(solution)/shard_map/pallas_call | solution.py:433
Async XLA Ops:
  0.6 19.1 %copy-start = (bf16[768,4,32]{0,2,1:T(8,128)(2,1)S(1)}, bf16[768,4,32]{0,2,1:T(8,128)(2,1)}, u32[]{:S(2)}) copy-start(bf16[768,4,32]{0,2,1:T(8,128)(2,1)} %param.19) | copy-start | bytes 589828
  2.4 11.0 %copy-start.2 = (bf16[32,128]{1,0:T(8,128)(2,1)}, bf16[32,128]{1,0:T(8,128)(2,1)S(1)}, u32[]{:S(2)}) copy-start(bf16[32,128]{1,0:T(8,128)(2,1)S(1)} %get-tuple-element.36.early) | copy-start | bytes 24580
  2.4 17.4 %collective-permute-start = (bf16[544,128]{1,0:T(8,128)(2,1)S(1)}, bf16[544,128]{1,0:T(8,128)(2,1)S(1)}, u32[]{:S(2)}, u32[]{:S(2)}) collective-permute-start(bf16[544,128]{1,0:T(8,128)(2,1)S(1)} %get-tuple-element.38), channel_id=1, source_target_pairs={{0,254},{1,255},{2,4},{3,5},{4,2},{5,3},{6,8},{7,9},{8,6},{9,7},{1... | collective-permute-start | bytes 417800 | tf_op jit(solution)/shard_map/ppermute | solution.py:336
  10.6 9.2 %collective-permute-start.2 = (bf16[544,128]{1,0:T(8,128)(2,1)S(1)}, bf16[544,128]{1,0:T(8,128)(2,1)S(1)}, u32[]{:S(2)}, u32[]{:S(2)}) collective-permute-start(bf16[544,128]{1,0:T(8,128)(2,1)S(1)} %get-tuple-element.40), channel_id=1, source_target_pairs={{0,2},{1,3},{2,0},{3,1},{4,6},{5,7},{6,4},{7,5},{8,10},{9,11},{10,... | collective-permute-start | bytes 417800 | tf_op jit(solution)/shard_map/ppermute | solution.py:336
  10.6 9.2 %collective-permute-start.1 = (bf16[272,128]{1,0:T(8,128)(2,1)S(1)}, bf16[272,128]{1,0:T(8,128)(2,1)S(1)}, u32[]{:S(2)}, u32[]{:S(2)}) collective-permute-start(bf16[272,128]{1,0:T(8,128)(2,1)S(1)} %get-tuple-element.39), channel_id=1, source_target_pairs={{0,1},{1,0},{2,3},{3,2},{4,5},{5,4},{6,7},{7,6},{8,9},{9,8},{10,11... | collective-permute-start | bytes 208904 | tf_op jit(solution)/shard_map/ppermute | solution.py:326
  11.6 6.0 %collective-permute-start.3 = (bf16[32,128]{1,0:T(8,128)(2,1)S(1)}, bf16[32,128]{1,0:T(8,128)(2,1)S(1)}, u32[]{:S(2)}, u32[]{:S(2)}) collective-permute-start(bf16[32,128]{1,0:T(8,128)(2,1)S(1)} %get-tuple-element.36.early), channel_id=1, source_target_pairs={{0,3},{1,2},{2,1},{3,0},{4,7},{5,6},{6,5},{7,4},{8,11},{9,10},{10,... | collective-permute-start | bytes 24584 | tf_op jit(solution)/shard_map/ppermute | solution.py:336
  12.5 7.3 %collective-permute-start.4 = (bf16[32,128]{1,0:T(8,128)(2,1)S(1)}, bf16[32,128]{1,0:T(8,128)(2,1)S(1)}, u32[]{:S(2)}, u32[]{:S(2)}) collective-permute-start(bf16[32,128]{1,0:T(8,128)(2,1)S(1)} %get-tuple-element.41), channel_id=1, source_target_pairs={{0,255},{1,254},{2,5},{3,4},{4,3},{5,2},{6,9},{7,8},{8,7},{9,6},{1... | collective-permute-start | bytes 24584 | tf_op jit(solution)/shard_map/ppermute | solution.py:336
  13.4 0.7 %copy-start.1 = (f32[4,768]{1,0:T(4,128)S(1)}, f32[4,768]{1,0:T(4,128)}, u32[]{:S(2)}) copy-start(f32[4,768]{1,0:T(4,128)} %b_mid.1) | copy-start | bytes 36868
  19.8 14.5 %collective-permute-start.6 = (bf16[128,768]{1,0:T(8,128)(2,1)S(1)}, bf16[128,768]{1,0:T(8,128)(2,1)S(1)}, u32[]{:S(2)}, u32[]{:S(2)}) collective-permute-start(bf16[128,768]{1,0:T(8,128)(2,1)S(1)} %bitcast.8), channel_id=1, source_target_pairs={{0,1},{1,0},{2,3},{3,2},{4,5},{5,4},{6,7},{7,6},{8,9},{9,8},{10,11... | collective-permute-start | bytes 589832 | tf_op jit(solution)/shard_map/ppermute | solution.py:326
  29.3 5.0 %collective-permute-start.9 = (bf16[256,128]{1,0:T(8,128)(2,1)S(1)}, bf16[256,128]{1,0:T(8,128)(2,1)S(1)}, u32[]{:S(2)}, u32[]{:S(2)}) collective-permute-start(bf16[256,128]{1,0:T(8,128)(2,1)S(1)} %get-tuple-element.64), channel_id=1, source_target_pairs={{0,1},{1,0},{2,3},{3,2},{4,5},{5,4},{6,7},{7,6},{8,9},{9,8},{10,11... | collective-permute-start | bytes 196616 | tf_op jit(solution)/shard_map/ppermute | solution.py:326
  29.4 8.1 %collective-permute-start.8 = (bf16[256,128]{1,0:T(8,128)(2,1)S(1)}, bf16[256,128]{1,0:T(8,128)(2,1)S(1)}, u32[]{:S(2)}, u32[]{:S(2)}) collective-permute-start(bf16[256,128]{1,0:T(8,128)(2,1)S(1)} %get-tuple-element.61), channel_id=1, source_target_pairs={{0,1},{1,0},{2,3},{3,2},{4,5},{5,4},{6,7},{7,6},{8,9},{9,8},{10,11... | collective-permute-start | bytes 196616 | tf_op jit(solution)/shard_map/ppermute | solution.py:326
  31.4 11.2 %collective-permute-start.7 = (bf16[256,128]{1,0:T(8,128)(2,1)S(1)}, bf16[256,128]{1,0:T(8,128)(2,1)S(1)}, u32[]{:S(2)}, u32[]{:S(2)}) collective-permute-start(bf16[256,128]{1,0:T(8,128)(2,1)S(1)} %get-tuple-element.58), channel_id=1, source_target_pairs={{0,1},{1,0},{2,3},{3,2},{4,5},{5,4},{6,7},{7,6},{8,9},{9,8},{10,11... | collective-permute-start | bytes 196616 | tf_op jit(solution)/shard_map/ppermute | solution.py:326
  31.5 14.2 %collective-permute-start.5 = (bf16[256,128]{1,0:T(8,128)(2,1)S(1)}, bf16[256,128]{1,0:T(8,128)(2,1)S(1)}, u32[]{:S(2)}, u32[]{:S(2)}) collective-permute-start(bf16[256,128]{1,0:T(8,128)(2,1)S(1)} %get-tuple-element.50), channel_id=1, source_target_pairs={{0,1},{1,0},{2,3},{3,2},{4,5},{5,4},{6,7},{7,6},{8,9},{9,8},{10,11... | collective-permute-start | bytes 196616 | tf_op jit(solution)/shard_map/ppermute | solution.py:326
  37.4 13.3 %collective-permute-start.13 = (bf16[256,128]{1,0:T(8,128)(2,1)S(1)}, bf16[256,128]{1,0:T(8,128)(2,1)S(1)}, u32[]{:S(2)}, u32[]{:S(2)}) collective-permute-start(bf16[256,128]{1,0:T(8,128)(2,1)S(1)} %get-tuple-element.69), channel_id=1, source_target_pairs={{0,1},{1,0},{2,3},{3,2},{4,5},{5,4},{6,7},{7,6},{8,9},{9,8},{10,11... | collective-permute-start | bytes 196616 | tf_op jit(solution)/shard_map/ppermute | solution.py:326
  40.5 10.2 %collective-permute-start.12 = (bf16[256,128]{1,0:T(8,128)(2,1)S(1)}, bf16[256,128]{1,0:T(8,128)(2,1)S(1)}, u32[]{:S(2)}, u32[]{:S(2)}) collective-permute-start(bf16[256,128]{1,0:T(8,128)(2,1)S(1)} %get-tuple-element.68), channel_id=1, source_target_pairs={{0,1},{1,0},{2,3},{3,2},{4,5},{5,4},{6,7},{7,6},{8,9},{9,8},{10,11... | collective-permute-start | bytes 196616 | tf_op jit(solution)/shard_map/ppermute | solution.py:326
  45.5 5.2 %collective-permute-start.11 = (bf16[256,128]{1,0:T(8,128)(2,1)S(1)}, bf16[256,128]{1,0:T(8,128)(2,1)S(1)}, u32[]{:S(2)}, u32[]{:S(2)}) collective-permute-start(bf16[256,128]{1,0:T(8,128)(2,1)S(1)} %get-tuple-element.67), channel_id=1, source_target_pairs={{0,1},{1,0},{2,3},{3,2},{4,5},{5,4},{6,7},{7,6},{8,9},{9,8},{10,11... | collective-permute-start | bytes 196616 | tf_op jit(solution)/shard_map/ppermute | solution.py:326
  48.6 4.4 %collective-permute-start.10 = (bf16[256,128]{1,0:T(8,128)(2,1)S(1)}, bf16[256,128]{1,0:T(8,128)(2,1)S(1)}, u32[]{:S(2)}, u32[]{:S(2)}) collective-permute-start(bf16[256,128]{1,0:T(8,128)(2,1)S(1)} %get-tuple-element.66), channel_id=1, source_target_pairs={{0,1},{1,0},{2,3},{3,2},{4,5},{5,4},{6,7},{7,6},{8,9},{9,8},{10,11... | collective-permute-start | bytes 196616 | tf_op jit(solution)/shard_map/ppermute | solution.py:326
